TPU v7x, 512 devices: a whole 4x4x16 slice. The times are simulated.
512 devices in a mesh: dp: 64 (over z, y_lo, core), tensor: 8 (over x, y_hi).
Axes of the slice: x: 4, y: 4 (y_hi: 2, y_lo: 2; y = y_hi * 2 + y_lo), z: 16, core: 2. Of those that a mesh axis runs over, the one named last changes fastest.
Arguments:
- activations: bfloat16 [98304, 2048], P('dp', 'tensor'), may hold values from -6 to 6
- out_grads: bfloat16 [98304, 2048], P('dp', 'tensor'), may hold values from -0.001953125 to 0.001953125
- left_stat: float32 [2048, 2048], P('dp', 'tensor'), may hold values from -1 to 11, as said below
- right_stat: float32 [2048, 2048], P('dp', 'tensor'), may hold values from -1 to 11, as said below
Outputs:
- left_new: float32 [2048, 2048], P('dp', 'tensor')
- right_new: float32 [2048, 2048], P('dp', 'tensor')
- update: float32 [2048, 2048], P('dp', 'tensor')
Inputs may be any that keep to these rules, and one draw needn't show every extreme that they name: `left_stat`: symmetric, with a positive diagonal. `right_stat`: symmetric, with a positive diagonal.
All inputs are finite; a program needn't handle non-finite values.
Results may differ from a plain program's by a relative error of at most 0.0012.
Values may be sent and summed in bfloat16 or wider, within the bound.
A program may use at most 64 MiB of HBM per device.

v0:
```python
import jax
import jax.numpy as jnp
from jax import lax
from jax.sharding import Mesh
from jax.sharding import PartitionSpec as P

TENSOR = ("tensor_0", "tensor_1")
DP = ("dp_0", "dp_1", "dp_2")
DP_TENSOR = ("dp_0", "dp_1", "dp_2", "tensor_0", "tensor_1")


def in_blocks(x, dim, length):
    lengths = x.shape
    blocks = x.reshape(*lengths[:dim], length, lengths[dim] // length, *lengths[dim + 1 :])
    return jnp.moveaxis(blocks, dim, 0)


def sum_at_owner(x, axis, dim):
    length = lax.axis_size(axis)
    blocks = lax.all_to_all(in_blocks(x, dim, length), axis, 0, 0, tiled=True)
    return jnp.sum(blocks, axis=0)


def in_order(blocks, dim):
    blocks = jnp.moveaxis(blocks, 0, dim)
    lengths = blocks.shape
    return blocks.reshape(*lengths[:dim], lengths[dim] * lengths[dim + 1], *lengths[dim + 2 :])


def gather_in_order(x, axes, turns):
    blocks = x
    for k in turns:
        blocks = lax.all_gather(blocks, axes[k])
    done = turns[::-1]
    back = [done.index(k) for k in range(len(axes))]
    blocks = blocks.transpose(*back, *range(len(axes), blocks.ndim))
    return blocks.reshape(-1, *x.shape)


def gathered_by_axis(x, axes, turns, dim):
    return in_order(gather_in_order(x, axes, turns), dim)


def side_by_side(arrays, axis, dim, along):
    both = jnp.concatenate(arrays, axis=along)
    result, at, gathered = (sum_at_owner(both, axis, dim), 0, [])
    for a in arrays:
        gathered.append(lax.slice_in_dim(result, at, at + a.shape[along], axis=along))
        at += a.shape[along]
    return tuple(gathered)


def by_axis(x, axes):
    for axis in axes:
        x = lax.psum(x, axis)
    return x


def sent_to_all(x, axis):
    length = lax.axis_size(axis)
    return lax.all_to_all(jnp.broadcast_to(x[None], (length, *x.shape)), axis, 0, 0, tiled=True)


def gather_directly(x, axis, dim):
    return in_order(sent_to_all(x, axis), dim)


def local(activations, out_grads, left_stat, right_stat):
    highest = lax.Precision.HIGHEST
    tensor_count = lax.axis_size(TENSOR)
    dp_count = lax.axis_size(DP)
    col_count = out_grads.shape[1]
    full_order = col_count * tensor_count
    row_count = full_order // dp_count
    grad_terms = lax.dot_general(
        lax.all_gather(activations, TENSOR, axis=1, tiled=True),
        out_grads,
        (((0,), (0,)), ((), ())),
        preferred_element_type=jnp.float32,
    )
    grad_block = sum_at_owner(grad_terms, DP, 0)
    grad_cols = gathered_by_axis(grad_block, DP, (1, 0, 2), 0)
    left_part = lax.dot_general(
        grad_block,
        grad_cols,
        (((1,), (1,)), ((), ())),
        precision=highest,
        preferred_element_type=jnp.float32,
    )
    dp_place = lax.axis_index(DP)
    row_start = dp_place * row_count
    tensor_rows = lax.all_to_all(grad_cols, TENSOR, split_axis=0, concat_axis=1, tiled=True)
    strip_cols = lax.dynamic_slice_in_dim(tensor_rows, row_start, row_count, 1)
    right_part = lax.dot_general(
        strip_cols,
        tensor_rows,
        (((0,), (0,)), ((), ())),
        precision=highest,
        preferred_element_type=jnp.float32,
    )
    left_sum, right_sum = side_by_side((left_part, right_part), TENSOR, 1, 0)
    left_new = 0.9 * left_stat + 0.1 * left_sum
    right_new = 0.9 * right_stat + 0.1 * right_sum
    left_sq = jnp.sum(left_new * left_new)
    right_sq = jnp.sum(right_new * right_new)
    grad_sq = jnp.sum(grad_block * grad_block)
    left_total, right_total, grad_total = (
        by_axis(left_sq, DP_TENSOR),
        by_axis(right_sq, DP_TENSOR),
        by_axis(grad_sq, DP_TENSOR),
    )
    left_scale = jnp.sqrt(left_total / full_order + 1e-06)
    right_scale = jnp.sqrt(right_total / full_order + 1e-06)
    left_whole = gather_directly(left_new, TENSOR, 1)
    left_product = jnp.dot(
        left_whole, grad_cols, precision=highest, preferred_element_type=jnp.float32
    )
    pre_left = 5.0 * grad_block - left_product / left_scale
    pre_rows = gather_directly(pre_left, TENSOR, 1)
    right_product = jnp.dot(
        pre_rows,
        lax.all_gather(right_new.astype(jnp.bfloat16), DP, axis=0, tiled=True).astype(jnp.float32),
        precision=highest,
        preferred_element_type=jnp.float32,
    )
    pre_block = 5.0 * pre_left - right_product / right_scale
    pre_sq = jnp.sum(pre_block * pre_block)
    pre_total = by_axis(pre_sq, DP_TENSOR)
    factor = jnp.sqrt(grad_total + 1e-06) / jnp.sqrt(pre_total + 1e-06)
    return (left_new, right_new, pre_block * factor)


def solution(mesh):
    finer = Mesh(
        mesh.devices.reshape(16, 2, 2, 4, 2), ("dp_0", "dp_1", "dp_2", "tensor_0", "tensor_1")
    )
    placed = (P(DP, TENSOR), P(DP, TENSOR), P(DP, TENSOR), P(DP, TENSOR))
    return jax.shard_map(
        local,
        mesh=finer,
        in_specs=placed,
        out_specs=(P(DP, TENSOR), P(DP, TENSOR), P(DP, TENSOR)),
        check_vma=False,
    )
```

profile of v0, /device:TPU:16, one launch (start us, length us, event | category | flops | bytes accessed | tf_op | source)
XLA Modules:
  0.0 582.7 jit_solution(15723450914595324753)
XLA Ops:
  8.0 119.7 %all-gather.8.cloned.1.call-done = bf16[1536,2048]{1,0:T(8,128)(2,1)} async-done(((bf16[1536,256]{1,0:T(8,128)(2,1)}), bf16[1536,2048]{1,0:T(8,128)(2,1)}) %all-gather.8.cloned.1.call-update) | async-done | bytes 6291472 | tf_op jit(solution)/shard_map/all_gather | solution.py:76
  127.6 4.7 fusion.10
  132.4 115.6 %all_to_all.39 = f32[64,32,256]{2,1,0:T(8,128)S(1)} all-to-all(f32[64,32,256]{2,1,0:T(8,128)S(1)} %bitcast.35), channel_id=1, replica_groups=mesh['dp_0'=16,'dp_1'=2,'dp_2'=2,'tensor_0'=4,'tensor_1'=2] {'dp_0','dp_..., dimensions={0} | all-to-all | bytes 4194304 | tf_op jit(solution)/shard_map/all_to_all | solution.py:20
  248.1 4.7 all-gather
  252.9 61.7 %all-gather.12.cloned.1.call-done = f32[32,32,256]{2,1,0:T(8,128)} async-done(((f32[2,32,256]{2,1,0:T(8,128)}), f32[32,32,256]{2,1,0:T(8,128)}) %all-gather.12.cloned.1.call-update) | async-done | bytes 1048592 | tf_op jit(solution)/shard_map/all_gather | solution.py:33
  314.6 20.0 %all-gather.14.cloned.1.call-done = f32[32,2,32,256]{3,2,1,0:T(8,128)} async-done(((f32[16,2,32,256]{3,2,1,0:T(8,128)}), f32[32,2,32,256]{3,2,1,0:T(8,128)}) %all-gather.14.cloned.1.call-update) | async-done | bytes 2097168 | tf_op jit(solution)/shard_map/all_gather | solution.py:33
  334.6 3.2 copy.11
  337.8 7.2 %all-to-all-start.1 = ((f32[8,256,256]{2,1,0:T(8,128)}), f32[8,256,256]{2,1,0:T(8,128)S(1)}, u32[]{:S(2)}, u32[]{:S(2)}) async-start(f32[8,256,256]{2,1,0:T(8,128)} %bitcast.7), calls=%async_computation.1 | async-start | bytes 4194304 | tf_op jit(solution)/shard_map/all_to_all | solution.py:92
  345.0 3.6 fusion.11
  348.7 27.0 %all-to-all-done.1 = f32[8,256,256]{2,1,0:T(8,128)S(1)} async-done(((f32[8,256,256]{2,1,0:T(8,128)}), f32[8,256,256]{2,1,0:T(8,128)S(1)}, u32[]{:S(2)}, u32[]{:S(2)}) %all-to-all-start.1) | async-done | bytes 2097184 | tf_op jit(solution)/shard_map/all_to_all | solution.py:92
  375.6 1.3 copy-done.1
  376.9 1.9 copy.13
  378.9 2.0 fusion.4
  381.0 13.0 %all_to_all.40 = f32[8,64,256]{2,1,0:T(8,128)S(1)} all-to-all(f32[8,64,256]{2,1,0:T(8,128)S(1)} %bitcast.37), channel_id=1, replica_groups=mesh['dp_0'=16,'dp_1'=2,'dp_2'=2,'tensor_0'=4,'tensor_1'=2] {'tensor_0',..., dimensions={0} | all-to-all | bytes 1048576 | tf_op jit(solution)/shard_map/all_to_all | solution.py:20
  394.0 1.2 fusion.7
  395.3 0.7 broadcast_in_dim.4
  396.0 5.6 all-to-all-start.3
  402.3 32.0 %all-reduce.1 = (f32[]{:T(128)}, f32[]{:T(128)}) all-reduce(f32[]{:T(128)} %get-tuple-element.27, f32[]{:T(128)} %multiply_reduce_fusion.2), channel_id=1, replica_groups=mesh['dp_0'=16,'dp_1'=2,'dp_2'=2,'tensor_0'=4,'tensor_1'=2] {'dp_0'}, use_global_device_ids=true, to_apply=%region_3.0 | all-reduce | flops 2 | bytes 16 | tf_op jit(solution)/shard_map/psum | solution.py:55
  434.3 5.6 all-reduce.9
  439.9 3.2 all-reduce.7
  443.1 11.1 %all-reduce.3 = (f32[]{:T(128)}, f32[]{:T(128)}) all-reduce(f32[]{:T(128)} %get-tuple-element.17, f32[]{:T(128)} %get-tuple-element.18), channel_id=1, replica_groups=mesh['dp_0'=16,'dp_1'=2,'dp_2'=2,'tensor_0'=4,'tensor_1'=2] {'tensor_0'}, use_global_device_ids=true, to_apply=%region_6.0 | all-reduce | flops 2 | bytes 16 | tf_op jit(solution)/shard_map/psum | solution.py:55
  454.2 7.1 %all-reduce.5 = (f32[]{:T(128)}, f32[]{:T(128)}) all-reduce(f32[]{:T(128)} %get-tuple-element.9, f32[]{:T(128)} %get-tuple-element.10), channel_id=1, replica_groups=mesh['dp_0'=16,'dp_1'=2,'dp_2'=2,'tensor_0'=4,'tensor_1'=2] {'tensor_1'}, use_global_device_ids=true, to_apply=%region_7.0 | all-reduce | flops 2 | bytes 16 | tf_op jit(solution)/shard_map/psum | solution.py:55
  462.1 2.7 fusion.1
  465.5 5.1 all-to-all-start.4
  471.8 4.9 all-to-all-done.4
  476.8 38.5 %all-gather.10.cloned.1.call-done = bf16[2048,256]{1,0:T(8,128)(2,1)} async-done(((bf16[32,256]{1,0:T(8,128)(2,1)}), bf16[2048,256]{1,0:T(8,128)(2,1)}) %all-gather.10.cloned.1.call-update) | async-done | bytes 1048592 | tf_op jit(solution)/shard_map/all_gather | solution.py:122
  515.3 2.4 multiply_reduce_fusion
  517.7 29.6 %all-reduce = (f32[]{:T(128)}, f32[]{:T(128)}) all-reduce(f32[]{:T(128)} %multiply_reduce_fusion.1, f32[]{:T(128)} %get-tuple-element.29), channel_id=1, replica_groups=mesh['dp_0'=16,'dp_1'=2,'dp_2'=2,'tensor_0'=4,'tensor_1'=2] {'dp_0'}, use_global_device_ids=true, to_apply=%region_15.0 | all-reduce | flops 2 | bytes 16 | tf_op jit(solution)/shard_map/psum | solution.py:55
  547.4 5.6 all-reduce.8
  553.0 3.1 all-reduce.6
  556.1 11.2 %all-reduce.2 = (f32[]{:T(128)}, f32[]{:T(128)}) all-reduce(f32[]{:T(128)} %get-tuple-element.15, f32[]{:T(128)} %get-tuple-element.16), channel_id=1, replica_groups=mesh['dp_0'=16,'dp_1'=2,'dp_2'=2,'tensor_0'=4,'tensor_1'=2] {'tensor_0'}, use_global_device_ids=true, to_apply=%region_18.0 | all-reduce | flops 2 | bytes 16 | tf_op jit(solution)/shard_map/psum | solution.py:55
  567.2 7.1 %all-reduce.4 = (f32[]{:T(128)}, f32[]{:T(128)}) all-reduce(f32[]{:T(128)} %get-tuple-element.7, f32[]{:T(128)} %get-tuple-element.8), channel_id=1, replica_groups=mesh['dp_0'=16,'dp_1'=2,'dp_2'=2,'tensor_0'=4,'tensor_1'=2] {'tensor_1'}, use_global_device_ids=true, to_apply=%region_19.0 | all-reduce | flops 2 | bytes 16 | tf_op jit(solution)/shard_map/psum | solution.py:55
  (30 shorter events, 3.7 us)
Async XLA Ops:
  7.2 120.5 %copy-start = (bf16[1536,256]{1,0:T(8,128)(2,1)S(1)}, bf16[1536,256]{1,0:T(8,128)(2,1)}, u32[]{:S(2)}) copy-start(bf16[1536,256]{1,0:T(8,128)(2,1)} %param.5) | copy-start | bytes 2359300
  7.2 120.4 %all-gather.8.cloned.1.call-start = ((), (), s32[]{:S(2)}) async-start(), calls=%async_computation.5 | async-start | bytes 7077888 | tf_op jit(solution)/shard_map/all_gather | solution.py:76
  7.9 306.7 %all-gather.12.cloned.1.call-start = ((), (), s32[]{:S(2)}) async-start(), calls=%async_computation.7 | async-start | bytes 1114112 | tf_op jit(solution)/shard_map/all_gather | solution.py:33
  252.8 81.8 %all-gather.14.cloned.1.call-start = ((), (), s32[]{:S(2)}) async-start(), calls=%async_computation.8 | async-start | bytes 3145728 | tf_op jit(solution)/shard_map/all_gather | solution.py:33
  337.8 37.8 %all-to-all-start.1 = ((f32[8,256,256]{2,1,0:T(8,128)}), f32[8,256,256]{2,1,0:T(8,128)S(1)}, u32[]{:S(2)}, u32[]{:S(2)}) async-start(f32[8,256,256]{2,1,0:T(8,128)} %bitcast.7), calls=%async_computation.1 | async-start | bytes 4194304 | tf_op jit(solution)/shard_map/all_to_all | solution.py:92
  345.0 170.2 %all-gather.10.cloned.1.call-start = ((), (), s32[]{:S(2)}) async-start(), calls=%async_computation.6 | async-start | bytes 1064960 | tf_op jit(solution)/shard_map/all_gather | solution.py:122
  375.6 1.3 copy-start.1
  380.9 13.1 %copy-start.4 = (f32[32,256]{1,0:T(8,128)S(1)}, f32[32,256]{1,0:T(8,128)}, u32[]{:S(2)}) copy-start(f32[32,256]{1,0:T(8,128)} %param.7) | copy-start | bytes 98308
  380.9 13.1 %copy-start.5 = (f32[32,256]{1,0:T(8,128)S(1)}, f32[32,256]{1,0:T(8,128)}, u32[]{:S(2)}) copy-start(f32[32,256]{1,0:T(8,128)} %param.6) | copy-start | bytes 98308
  395.2 70.3 %copy-start.2 = (f32[32,256]{1,0:T(8,128)}, f32[32,256]{1,0:T(8,128)S(1)}, u32[]{:S(2)}) copy-start(f32[32,256]{1,0:T(8,128)S(1)} %get-tuple-element.28) | copy-start | bytes 98308
  395.2 70.3 %copy-start.3 = (f32[32,256]{1,0:T(8,128)}, f32[32,256]{1,0:T(8,128)S(1)}, u32[]{:S(2)}) copy-start(f32[32,256]{1,0:T(8,128)S(1)} %get-tuple-element.24) | copy-start | bytes 98308
  396.0 66.1 %all-to-all-start.3 = ((f32[8,32,256]{2,1,0:T(8,128)}), f32[8,32,256]{2,1,0:T(8,128)S(1)}, u32[]{:S(2)}, u32[]{:S(2)}) async-start(f32[8,32,256]{2,1,0:T(8,128)} %broadcast_in_dim.4), calls=%async_computation.3 | async-start | bytes 524288 | tf_op jit(solution)/shard_map/all_to_all | solution.py:61
  465.5 11.2 %all-to-all-start.4 = ((f32[8,32,256]{2,1,0:T(8,128)}), f32[8,32,256]{2,1,0:T(8,128)S(1)}, u32[]{:S(2)}, u32[]{:S(2)}) async-start(f32[8,32,256]{2,1,0:T(8,128)} %broadcast_in_dim.5), calls=%async_computation.4 | async-start | bytes 524288 | tf_op jit(solution)/shard_map/all_to_all | solution.py:61
Sparse Core Ops, SparseCore 0:
  11.1 116.5 all-gather.7
  253.0 61.5 all-gather.11
  316.7 17.9 all-gather.13
  395.4 119.8 all-gather.9
where the time goes:
time: 584 us; the launch traced here: 583 us
  waiting for transfers between devices  273 us (47%)
  blocking collectives  249 us (43%)
  starting transfers between devices  18.1 us (3%)
  between operations  16.5 us (3%)
  matrix products  15.5 us (3%)
  local copies, waits for them, and re-layouts  7.96 us (1%)
    all_to_all x2, blocking collectives, sum_at_owner(): blocks = lax.all_to_all(in_blocks(x, dim, length), axis, 0, 0, tiled=True)  129 us
    all_gather x1, waiting for transfers between devices, local(): lax.all_gather(activations, TENSOR, axis=1, tiled=True)  120 us
    psum x10, blocking collectives, by_axis(): x = lax.psum(x, axis)  116 us
    all_gather x2, waiting for transfers between devices, gather_in_order(): blocks = lax.all_gather(blocks, axes[k])  81.7 us
    all_gather x1, waiting for transfers between devices, local(): lax.all_gather(right_new.astype(jnp.bfloat16), DP, axis=0, tiled=True)  38.5 us
    all_to_all x1, waiting for transfers between devices, local(): lax.all_to_all(grad_cols, TENSOR, split_axis=0, concat_axis=1, tiled=True)  27 us
  transfers between devices with their start and end apart: 7, of which 6 were waited for; matrix products, arithmetic and copies ran while one was open for 2% of the time, Pallas kernels for 0%

commit v1 on v0

--- a/solution.py
+++ b/solution.py
@@ -72,8 +72,18 @@
     col_count = out_grads.shape[1]
     full_order = col_count * tensor_count
     row_count = full_order // dp_count
+
+    def groups_raise(mine_x):
+        h_now = jnp.concatenate(
+            lax.all_to_all(
+                jnp.stack([mine_x for _ in range(lax.axis_size(TENSOR))], 0), TENSOR, 0, 0
+            ),
+            axis=1,
+        )
+        return h_now
+
     grad_terms = lax.dot_general(
-        lax.all_gather(activations, TENSOR, axis=1, tiled=True),
+        groups_raise(activations),
         out_grads,
         (((0,), (0,)), ((), ())),
         preferred_element_type=jnp.float32,

time: 584 us -> 542 us (0.928)
  the two profiles are of different devices: /device:TPU:16 before, /device:TPU:8 now
where the time goes in v1:
time: 542 us; the launch traced here: 541 us
  blocking collectives  332 us (61%)
  waiting for transfers between devices  153 us (28%)
  between operations  16.5 us (3%)
  starting transfers between devices  13.9 us (3%)
  matrix products  12.5 us (2%)
  local copies, waits for them, and re-layouts  9.96 us (2%)
    all_to_all x2, blocking collectives, sum_at_owner(): blocks = lax.all_to_all(in_blocks(x, dim, length), axis, 0, 0, tiled=True)  132 us
    psum x10, blocking collectives, by_axis(): x = lax.psum(x, axis)  116 us
    all_gather x2, waiting for transfers between devices, gather_in_order(): blocks = lax.all_gather(blocks, axes[k])  79.6 us
    all_to_all x1, blocking collectives, groups_raise(): lax.all_to_all(jnp.stack([mine_x for _ in range(lax.axis_size(TENSOR))],...  79.4 us
    all_gather x1, waiting for transfers between devices, local(): lax.all_gather(right_new.astype(jnp.bfloat16), DP, axis=0, tiled=True)  37.4 us
    all_to_all x1, waiting for transfers between devices, local(): lax.all_to_all(grad_cols, TENSOR, split_axis=0, concat_axis=1, tiled=True)  28.2 us
  transfers between devices with their start and end apart: 6, of which 5 were waited for; matrix products, arithmetic and copies ran while one was open for 2% of the time, Pallas kernels for 0%

profile of v1, /device:TPU:8, one launch (start us, length us, event | category | flops | bytes accessed | tf_op | source)
XLA Modules:
  0.0 541.0 jit_solution(11380442194920835433)
XLA Ops:
  7.2 1.5 copy.14
  9.2 79.4 %all_to_all.44 = bf16[8,1536,256]{1,2,0:T(8,128)(2,1)S(1)} all-to-all(bf16[8,1536,256]{1,2,0:T(8,128)(2,1)S(1)} %stack.2), channel_id=1, replica_groups=mesh['dp_0'=16,'dp_1'=2,'dp_2'=2,'tensor_0'=4,'tensor_1'=2] {'tensor_0',..., dimensions={0} | all-to-all | bytes 12582912 | tf_op jit(solution)/shard_map/all_to_all | solution.py:78
  88.7 1.8 fusion.2
  90.5 117.9 %all_to_all.45 = f32[64,32,256]{2,1,0:T(8,128)S(1)} all-to-all(f32[64,32,256]{2,1,0:T(8,128)S(1)} %fusion.2), channel_id=1, replica_groups=mesh['dp_0'=16,'dp_1'=2,'dp_2'=2,'tensor_0'=4,'tensor_1'=2] {'dp_0','dp_..., dimensions={0} | all-to-all | bytes 4194304 | tf_op jit(solution)/shard_map/all_to_all | solution.py:20
  208.5 4.7 all-gather
  213.3 59.6 %all-gather.9.cloned.1.call-done = f32[32,32,256]{2,1,0:T(8,128)} async-done(((f32[2,32,256]{2,1,0:T(8,128)}), f32[32,32,256]{2,1,0:T(8,128)}) %all-gather.9.cloned.1.call-update) | async-done | bytes 1048592 | tf_op jit(solution)/shard_map/all_gather | solution.py:33
  273.0 20.0 %all-gather.11.cloned.1.call-done = f32[32,2,32,256]{3,2,1,0:T(8,128)} async-done(((f32[16,2,32,256]{3,2,1,0:T(8,128)}), f32[32,2,32,256]{3,2,1,0:T(8,128)}) %all-gather.11.cloned.1.call-update) | async-done | bytes 2097168 | tf_op jit(solution)/shard_map/all_gather | solution.py:33
  293.0 3.2 copy.15
  296.2 5.8 %all-to-all-start.2 = ((f32[8,256,256]{2,1,0:T(8,128)}), f32[8,256,256]{2,1,0:T(8,128)S(1)}, u32[]{:S(2)}, u32[]{:S(2)}) async-start(f32[8,256,256]{2,1,0:T(8,128)} %bitcast.11), calls=%async_computation.2 | async-start | bytes 4194304 | tf_op jit(solution)/shard_map/all_to_all | solution.py:102
  302.0 3.6 fusion.12
  305.6 28.2 %all-to-all-done.2 = f32[8,256,256]{2,1,0:T(8,128)S(1)} async-done(((f32[8,256,256]{2,1,0:T(8,128)}), f32[8,256,256]{2,1,0:T(8,128)S(1)}, u32[]{:S(2)}, u32[]{:S(2)}) %all-to-all-start.2) | async-done | bytes 2097184 | tf_op jit(solution)/shard_map/all_to_all | solution.py:102
  333.9 1.3 copy-done.1
  335.1 1.9 copy.17
  337.1 2.0 fusion.6
  339.2 14.0 %all_to_all.46 = f32[8,64,256]{2,1,0:T(8,128)S(1)} all-to-all(f32[8,64,256]{2,1,0:T(8,128)S(1)} %bitcast.45), channel_id=1, replica_groups=mesh['dp_0'=16,'dp_1'=2,'dp_2'=2,'tensor_0'=4,'tensor_1'=2] {'tensor_0',..., dimensions={0} | all-to-all | bytes 1048576 | tf_op jit(solution)/shard_map/all_to_all | solution.py:20
  353.3 1.2 fusion.9
  355.2 3.4 all-to-all-start.4
  359.3 32.0 %all-reduce.1 = (f32[]{:T(128)}, f32[]{:T(128)}) all-reduce(f32[]{:T(128)} %get-tuple-element.27, f32[]{:T(128)} %multiply_reduce_fusion.2), channel_id=1, replica_groups=mesh['dp_0'=16,'dp_1'=2,'dp_2'=2,'tensor_0'=4,'tensor_1'=2] {'dp_0'}, use_global_device_ids=true, to_apply=%region_3.0 | all-reduce | flops 2 | bytes 16 | tf_op jit(solution)/shard_map/psum | solution.py:55
  391.3 5.6 %all-reduce.9 = (f32[]{:T(128)}, f32[]{:T(128)}) all-reduce(f32[]{:T(128)} %get-tuple-element.5, f32[]{:T(128)} %get-tuple-element.6), channel_id=1, replica_groups=mesh['dp_0'=16,'dp_1'=2,'dp_2'=2,'tensor_0'=4,'tensor_1'=2] {'dp_1'}, use_global_device_ids=true, to_apply=%region_4.0 | all-reduce | flops 2 | bytes 16 | tf_op jit(solution)/shard_map/psum | solution.py:55
  397.0 3.2 all-reduce.7
  400.1 11.5 %all-reduce.3 = (f32[]{:T(128)}, f32[]{:T(128)}) all-reduce(f32[]{:T(128)} %get-tuple-element.17, f32[]{:T(128)} %get-tuple-element.18), channel_id=1, replica_groups=mesh['dp_0'=16,'dp_1'=2,'dp_2'=2,'tensor_0'=4,'tensor_1'=2] {'tensor_0'}, use_global_device_ids=true, to_apply=%region_6.0 | all-reduce | flops 2 | bytes 16 | tf_op jit(solution)/shard_map/psum | solution.py:55
  411.7 7.1 %all-reduce.5 = (f32[]{:T(128)}, f32[]{:T(128)}) all-reduce(f32[]{:T(128)} %get-tuple-element.9, f32[]{:T(128)} %get-tuple-element.10), channel_id=1, replica_groups=mesh['dp_0'=16,'dp_1'=2,'dp_2'=2,'tensor_0'=4,'tensor_1'=2] {'tensor_1'}, use_global_device_ids=true, to_apply=%region_7.0 | all-reduce | flops 2 | bytes 16 | tf_op jit(solution)/shard_map/psum | solution.py:55
  419.6 2.7 fusion.1
  423.0 4.6 all-to-all-start.5
  428.8 7.3 %all-to-all-done.5 = f32[8,32,256]{2,1,0:T(8,128)S(1)} async-done(((f32[8,32,256]{2,1,0:T(8,128)}), f32[8,32,256]{2,1,0:T(8,128)S(1)}, u32[]{:S(2)}, u32[]{:S(2)}) %all-to-all-start.5) | async-done | bytes 262176 | tf_op jit(solution)/shard_map/all_to_all | solution.py:61
  436.1 37.4 %all-gather.7.cloned.1.call-done = bf16[2048,256]{1,0:T(8,128)(2,1)} async-done(((bf16[32,256]{1,0:T(8,128)(2,1)}), bf16[2048,256]{1,0:T(8,128)(2,1)}) %all-gather.7.cloned.1.call-update) | async-done | bytes 1048592 | tf_op jit(solution)/shard_map/all_gather | solution.py:132
  473.5 2.4 multiply_reduce_fusion
  476.0 29.7 %all-reduce = (f32[]{:T(128)}, f32[]{:T(128)}) all-reduce(f32[]{:T(128)} %multiply_reduce_fusion.1, f32[]{:T(128)} %get-tuple-element.29), channel_id=1, replica_groups=mesh['dp_0'=16,'dp_1'=2,'dp_2'=2,'tensor_0'=4,'tensor_1'=2] {'dp_0'}, use_global_device_ids=true, to_apply=%region_15.0 | all-reduce | flops 2 | bytes 16 | tf_op jit(solution)/shard_map/psum | solution.py:55
  505.7 5.6 %all-reduce.8 = (f32[]{:T(128)}, f32[]{:T(128)}) all-reduce(f32[]{:T(128)} %get-tuple-element.3, f32[]{:T(128)} %get-tuple-element.4), channel_id=1, replica_groups=mesh['dp_0'=16,'dp_1'=2,'dp_2'=2,'tensor_0'=4,'tensor_1'=2] {'dp_1'}, use_global_device_ids=true, to_apply=%region_16.0 | all-reduce | flops 2 | bytes 16 | tf_op jit(solution)/shard_map/psum | solution.py:55
  511.3 3.1 all-reduce.6
  514.4 11.1 %all-reduce.2 = (f32[]{:T(128)}, f32[]{:T(128)}) all-reduce(f32[]{:T(128)} %get-tuple-element.15, f32[]{:T(128)} %get-tuple-element.16), channel_id=1, replica_groups=mesh['dp_0'=16,'dp_1'=2,'dp_2'=2,'tensor_0'=4,'tensor_1'=2] {'tensor_0'}, use_global_device_ids=true, to_apply=%region_18.0 | all-reduce | flops 2 | bytes 16 | tf_op jit(solution)/shard_map/psum | solution.py:55
  525.5 7.1 %all-reduce.4 = (f32[]{:T(128)}, f32[]{:T(128)}) all-reduce(f32[]{:T(128)} %get-tuple-element.7, f32[]{:T(128)} %get-tuple-element.8), channel_id=1, replica_groups=mesh['dp_0'=16,'dp_1'=2,'dp_2'=2,'tensor_0'=4,'tensor_1'=2] {'tensor_1'}, use_global_device_ids=true, to_apply=%region_19.0 | all-reduce | flops 2 | bytes 16 | tf_op jit(solution)/shard_map/psum | solution.py:55
  (30 shorter events, 4.3 us)
Async XLA Ops:
  7.2 81.5 %copy-start = (bf16[1536,256]{1,0:T(8,128)(2,1)S(1)}, bf16[1536,256]{1,0:T(8,128)(2,1)}, u32[]{:S(2)}) copy-start(bf16[1536,256]{1,0:T(8,128)(2,1)} %param.5) | copy-start | bytes 2359300
  7.2 265.7 %all-gather.9.cloned.1.call-start = ((), (), s32[]{:S(2)}) async-start(), calls=%async_computation.7 | async-start | bytes 1114112 | tf_op jit(solution)/shard_map/all_gather | solution.py:33
  213.3 79.7 %all-gather.11.cloned.1.call-start = ((), (), s32[]{:S(2)}) async-start(), calls=%async_computation.8 | async-start | bytes 3145728 | tf_op jit(solution)/shard_map/all_gather | solution.py:33
  296.2 37.7 %all-to-all-start.2 = ((f32[8,256,256]{2,1,0:T(8,128)}), f32[8,256,256]{2,1,0:T(8,128)S(1)}, u32[]{:S(2)}, u32[]{:S(2)}) async-start(f32[8,256,256]{2,1,0:T(8,128)} %bitcast.11), calls=%async_computation.2 | async-start | bytes 4194304 | tf_op jit(solution)/shard_map/all_to_all | solution.py:102
  302.0 171.6 %all-gather.7.cloned.1.call-start = ((), (), s32[]{:S(2)}) async-start(), calls=%async_computation.6 | async-start | bytes 1064960 | tf_op jit(solution)/shard_map/all_gather | solution.py:132
  333.9 1.3 copy-start.1
  339.1 14.2 %copy-start.4 = (f32[32,256]{1,0:T(8,128)S(1)}, f32[32,256]{1,0:T(8,128)}, u32[]{:S(2)}) copy-start(f32[32,256]{1,0:T(8,128)} %param.7) | copy-start | bytes 98308
  339.1 14.2 %copy-start.5 = (f32[32,256]{1,0:T(8,128)S(1)}, f32[32,256]{1,0:T(8,128)}, u32[]{:S(2)}) copy-start(f32[32,256]{1,0:T(8,128)} %param.6) | copy-start | bytes 98308
  354.5 68.5 %copy-start.2 = (f32[32,256]{1,0:T(8,128)}, f32[32,256]{1,0:T(8,128)S(1)}, u32[]{:S(2)}) copy-start(f32[32,256]{1,0:T(8,128)S(1)} %get-tuple-element.28) | copy-start | bytes 98308
  354.5 68.5 %copy-start.3 = (f32[32,256]{1,0:T(8,128)}, f32[32,256]{1,0:T(8,128)S(1)}, u32[]{:S(2)}) copy-start(f32[32,256]{1,0:T(8,128)S(1)} %get-tuple-element.24) | copy-start | bytes 98308
  355.2 64.3 %all-to-all-start.4 = ((f32[8,32,256]{2,1,0:T(8,128)}), f32[8,32,256]{2,1,0:T(8,128)S(1)}, u32[]{:S(2)}, u32[]{:S(2)}) async-start(f32[8,32,256]{2,1,0:T(8,128)} %broadcast_in_dim.4), calls=%async_computation.4 | async-start | bytes 524288 | tf_op jit(solution)/shard_map/all_to_all | solution.py:61
  423.0 13.1 %all-to-all-start.5 = ((f32[8,32,256]{2,1,0:T(8,128)}), f32[8,32,256]{2,1,0:T(8,128)S(1)}, u32[]{:S(2)}, u32[]{:S(2)}) async-start(f32[8,32,256]{2,1,0:T(8,128)} %broadcast_in_dim.5), calls=%async_computation.5 | async-start | bytes 524288 | tf_op jit(solution)/shard_map/all_to_all | solution.py:61
Sparse Core Ops, SparseCore 0:
  213.4 59.4 all-gather.8
  275.0 17.9 all-gather.10
  354.6 118.8 all-gather.6
